TPU v7x, 512 devices: a whole 4x8x8 slice. The times are simulated.
512 devices in a mesh: pp: 8 (over x, y_lo), ep: 64 (over z, y_hi, core).
Axes of the slice: x: 4, y: 8 (y_hi: 4, y_lo: 2; y = y_hi * 2 + y_lo), z: 8, core: 2. Of those that a mesh axis runs over, the one named last changes fastest.
Arguments:
- forward_acts: bfloat16 [8, 1536, 3584], P('pp', 'ep'), may hold values from -6 to 6
- backward_grads: bfloat16 [8, 1536, 3584], P('pp', 'ep'), may hold values from -6 to 6
- forward_routes: int32 [8, 1536, 2], P('pp', 'ep'), may hold values from 0 to 7, all different within a row; in each aligned block of 24 rows (0 to 23, 24 to 47, ..., all dimensions but the last counted through in order) at most 8 rows name the same one
- backward_routes: int32 [8, 1536, 2], P('pp', 'ep'), may hold values from 0 to 7, all different within a row; in each aligned block of 24 rows (0 to 23, 24 to 47, ..., all dimensions but the last counted through in order) at most 8 rows name the same one
- forward_gates: float32 [8, 1536, 2], P('pp', 'ep'), may hold values from 0.3 to 1.5
- backward_gates: float32 [8, 1536, 2], P('pp', 'ep'), may hold values from 0.3 to 1.5
- gate_weight: bfloat16 [8, 3584, 8192], P('pp', None, 'ep'), may hold values from -0.09375 to 0.09375
- up_weight: bfloat16 [8, 3584, 8192], P('pp', None, 'ep'), may hold values from -0.09375 to 0.09375
- down_weight: bfloat16 [8, 8192, 3584], P('pp', 'ep'), may hold values from -0.1875 to 0.1875
- stashed_pre: bfloat16 [8, 64, 64, 8, 2, 128], P('pp', 'ep'), may hold values from -5 to 5
Outputs:
- forward_next: bfloat16 [8, 1536, 3584], P('pp', 'ep')
- backward_next: bfloat16 [8, 1536, 3584], P('pp', 'ep')
Inputs may be any that keep to these rules, and one draw needn't show every extreme that they name: `forward_routes`: each token names 2 different experts; among the 24 tokens of one device at one section no expert is named more than 8 times, and some expert exactly that often. `backward_routes`: as for forward_routes.
All inputs are finite; a program needn't handle non-finite values.
Results may differ from a plain program's by a relative error of at most 0.0055.
Values may be sent and summed in bfloat16 or wider, within the bound.
A program may use at most 64 MiB of HBM per device.

v0:
```python
import jax
import jax.numpy as jnp
from jax import lax
from jax.sharding import PartitionSpec as P

GROUP = 8
TOPK = 2


def from_behind(value, axis, steps):
    count = lax.axis_size(axis)
    pairs = [(source, (source + steps) % count) for source in range(count)]
    return lax.ppermute(value, axis, pairs)


def route_tables(routes, gates, expert_count, capacity):
    token_count = routes.shape[0]
    expert_ids = routes.reshape(-1)
    columns = jnp.arange(expert_count, dtype=jnp.int32)
    onehot = (expert_ids[:, None] == columns[None, :]).astype(jnp.int32)
    earlier = jnp.cumsum(onehot, axis=0) - onehot
    slot_ids = jnp.sum(earlier * onehot, axis=1)
    target = expert_ids * capacity + slot_ids
    places = jnp.arange(expert_count * capacity, dtype=jnp.int32)
    picked = (target[:, None] == places[None, :]).astype(jnp.float32)
    picked = picked.reshape(token_count, TOPK, expert_count * capacity)
    plain = jnp.sum(picked, axis=1)
    weighted = jnp.sum(picked * gates[:, :, None], axis=1)
    return (plain, weighted)


def on_device(
    forward_acts,
    backward_grads,
    forward_routes,
    backward_routes,
    forward_gates,
    backward_gates,
    gate_weight,
    up_weight,
    down_weight,
    stashed_pre,
):
    ep_size = lax.axis_size("ep")
    expert_count = ep_size // GROUP
    capacity = stashed_pre.shape[3]
    width = forward_acts.shape[2]
    rows_total = ep_size * capacity
    acts = forward_acts[0]
    grads = backward_grads[0]
    plain_fwd, weighted_fwd = route_tables(
        forward_routes[0], forward_gates[0], expert_count, capacity
    )
    plain_bwd, weighted_bwd = route_tables(
        backward_routes[0], backward_gates[0], expert_count, capacity
    )
    leading = (((0,), (0,)), ((), ()))
    send_acts = lax.dot_general(
        plain_fwd.astype(jnp.bfloat16), acts, leading, preferred_element_type=jnp.float32
    ).astype(jnp.bfloat16)
    send_grads = lax.dot_general(
        weighted_bwd,
        grads.astype(jnp.float32),
        leading,
        precision=lax.Precision.HIGHEST,
        preferred_element_type=jnp.float32,
    ).astype(jnp.bfloat16)

    def widen(block):
        spread = jnp.broadcast_to(
            block.reshape(expert_count, 1, capacity, width), (expert_count, GROUP, capacity, width)
        )
        return spread.reshape(ep_size, capacity, width)

    arrived = (
        lax.all_to_all(widen(send_acts), "ep", split_axis=0, concat_axis=0, tiled=True),
        lax.all_to_all(widen(send_grads), "ep", split_axis=0, concat_axis=0, tiled=True),
    )
    rows_acts = arrived[0].reshape(rows_total, width)
    rows_grads = arrived[1].reshape(rows_total, width)
    gate_cols = gate_weight[0]
    up_cols = up_weight[0]
    down_rows = down_weight[0]
    hidden_dev = down_rows.shape[0]
    gate_value = jnp.dot(rows_acts, gate_cols, preferred_element_type=jnp.float32)
    up_value = jnp.dot(rows_acts, up_cols, preferred_element_type=jnp.float32)
    hidden = (jax.nn.silu(gate_value) * up_value).astype(jnp.bfloat16)
    out_part = jnp.dot(hidden, down_rows, preferred_element_type=jnp.float32).astype(jnp.bfloat16)
    trailing = (((1,), (1,)), ((), ()))
    hidden_grad = lax.dot_general(
        rows_grads, down_rows, trailing, preferred_element_type=jnp.float32
    )
    stashed = stashed_pre[0, 0].reshape(rows_total, 2, hidden_dev).astype(jnp.float32)
    gate_stash = stashed[:, 0, :]
    up_stash = stashed[:, 1, :]
    sigmoid_gate = jax.nn.sigmoid(gate_stash)
    gate_grad = (
        hidden_grad * up_stash * sigmoid_gate * (1.0 + gate_stash * (1.0 - sigmoid_gate))
    ).astype(jnp.bfloat16)
    up_grad = (hidden_grad * gate_stash * sigmoid_gate).astype(jnp.bfloat16)
    both_cols = jnp.concatenate([gate_cols, up_cols], axis=1)
    both_grads = jnp.concatenate([gate_grad, up_grad], axis=1)
    grad_part = lax.dot_general(
        both_grads, both_cols, trailing, preferred_element_type=jnp.float32
    ).astype(jnp.bfloat16)
    back = (
        lax.all_to_all(
            out_part.reshape(ep_size, capacity, width),
            "ep",
            split_axis=0,
            concat_axis=0,
            tiled=True,
        ),
        lax.all_to_all(
            grad_part.reshape(ep_size, capacity, width),
            "ep",
            split_axis=0,
            concat_axis=0,
            tiled=True,
        ),
    )
    summed = [
        jnp.sum(
            piece.astype(jnp.float32).reshape(expert_count, GROUP, capacity, width), axis=1
        ).reshape(expert_count * capacity, width)
        for piece in back
    ]
    routed = jnp.dot(
        weighted_fwd, summed[0], precision=lax.Precision.HIGHEST, preferred_element_type=jnp.float32
    )
    section_out = (acts.astype(jnp.float32) + routed).astype(jnp.bfloat16)
    returned = jnp.dot(
        plain_bwd, summed[1], precision=lax.Precision.HIGHEST, preferred_element_type=jnp.float32
    )
    section_grad = (grads.astype(jnp.float32) + returned).astype(jnp.bfloat16)
    moved = from_behind(jnp.stack([section_out, section_grad]), "pp", lax.axis_size("pp") - 1)
    return (moved[0][None], moved[1][None])


def solution(mesh):
    placed = (
        P("pp", "ep", None),
        P("pp", "ep", None),
        P("pp", "ep", None),
        P("pp", "ep", None),
        P("pp", "ep", None),
        P("pp", "ep", None),
        P("pp", None, "ep"),
        P("pp", None, "ep"),
        P("pp", "ep", None),
        P("pp", "ep", None, None, None, None),
    )
    return jax.shard_map(
        on_device,
        mesh=mesh,
        in_specs=placed,
        out_specs=(P("pp", "ep", None), P("pp", "ep", None)),
        check_vma=False,
    )
```

profile of v0, /device:TPU:104, one launch (start us, length us, event | category | flops | bytes accessed | tf_op | source)
XLA Modules:
  0.0 474.4 jit_solution(17298716373387014050)
XLA Ops:
  0.6 0.0 copy-start
  0.6 0.8 copy.34
  1.5 0.1 eq.58
  1.6 0.1 fusion.45
  1.7 0.1 reduce_window_sum.17
  1.7 0.2 select_reduce_fusion.3
  1.9 0.1 reduce_sum.77
  2.0 0.1 copy.35
  2.1 0.7 bitcast_add_fusion.1
  2.8 0.8 convert_reduce_fusion.3
  3.6 1.2 fusion.3
  4.8 2.1 broadcast_in_dim.9
  6.9 15.6 %all-to-all-start = ((bf16[64,8,3584]{2,1,0:T(8,128)(2,1)}), bf16[64,8,3584]{2,1,0:T(8,128)(2,1)}, u32[]{:S(2)}, u32[]{:S(2)}) async-start(bf16[64,8,3584]{2,1,0:T(8,128)(2,1)} %bitcast.93), calls=%async_computation | async-start | bytes 7340032 | tf_op jit(solution)/shard_map/all_to_all | solution.py:76
  22.5 0.0 copy-done.6
  22.5 0.1 copy.36
  22.6 0.1 eq.65
  22.7 0.1 fusion.44
  22.8 0.1 reduce_window_sum.18
  22.8 0.2 select_reduce_fusion.1
  23.0 0.1 reduce_sum.82
  23.1 0.1 copy.37
  23.2 0.0 copy-done.7
  23.2 0.1 select_reduce_fusion
  23.3 0.0 copy-done.4
  23.3 0.6 fusion.2
  23.9 83.1 %all-to-all-done = bf16[64,8,3584]{2,1,0:T(8,128)(2,1)} async-done(((bf16[64,8,3584]{2,1,0:T(8,128)(2,1)}), bf16[64,8,3584]{2,1,0:T(8,128)(2,1)}, u32[]{:S(2)}, u32[]{:S(2)}) %all-to-all-start) | async-done | bytes 3670048 | tf_op jit(solution)/shard_map/all_to_all | solution.py:76
  107.0 2.2 broadcast_in_dim.11
  109.2 12.9 %all-to-all-start.2 = ((bf16[64,8,3584]{2,1,0:T(8,128)(2,1)}), bf16[64,8,3584]{2,1,0:T(8,128)(2,1)}, u32[]{:S(2)}, u32[]{:S(2)}) async-start(bf16[64,8,3584]{2,1,0:T(8,128)(2,1)} %bitcast.94), calls=%async_computation.2 | async-start | bytes 7340032 | tf_op jit(solution)/shard_map/all_to_all | solution.py:77
  122.1 0.0 copy-done.2
  122.1 0.0 copy-start.1
  122.1 3.2 fusion.12
  125.4 0.0 copy-done
  125.4 7.8 %fusion = bf16[64,8,3584]{2,1,0:T(8,128)(2,1)} fusion(bf16[1,128,3584]{2,1,0:T(8,128)(2,1)S(1)} %copy-done, bf16[64,8,3584]{2,1,0:T(8,128)(2,1)} %all-to-all-done, f32[512,128]{1,0:T(8,128)S(1)} %fusion.12, bf16[1,3584,128]{2,1,0:T(8,128)(2,1)S(1)} %copy-done.1), kind=kOutput, calls=%fused_computation.4 | convolution fusion | flops 941752320 | bytes 9437184 | tf_op jit(solution)/shard_map/dot_general | solution.py:88
  133.2 84.3 %all-to-all-done.2 = bf16[64,8,3584]{2,1,0:T(8,128)(2,1)} async-done(((bf16[64,8,3584]{2,1,0:T(8,128)(2,1)}), bf16[64,8,3584]{2,1,0:T(8,128)(2,1)}, u32[]{:S(2)}, u32[]{:S(2)}) %all-to-all-start.2) | async-done | bytes 3670048 | tf_op jit(solution)/shard_map/all_to_all | solution.py:77
  217.4 25.6 %all-to-all-start.1 = ((bf16[64,8,3584]{2,1,0:T(8,128)(2,1)}), bf16[64,8,3584]{2,1,0:T(8,128)(2,1)}, u32[]{:S(2)}, u32[]{:S(2)}) async-start(bf16[64,8,3584]{2,1,0:T(8,128)(2,1)} %fusion), calls=%async_computation.1 | async-start | bytes 7340032 | tf_op jit(solution)/shard_map/all_to_all | solution.py:107
  243.0 3.1 fusion.32
  246.2 3.1 fusion.1
  249.2 83.6 %all-to-all-done.1 = bf16[64,8,3584]{2,1,0:T(8,128)(2,1)} async-done(((bf16[64,8,3584]{2,1,0:T(8,128)(2,1)}), bf16[64,8,3584]{2,1,0:T(8,128)(2,1)}, u32[]{:S(2)}, u32[]{:S(2)}) %all-to-all-start.1) | async-done | bytes 3670048 | tf_op jit(solution)/shard_map/all_to_all | solution.py:107
  332.9 16.5 %all-to-all-start.3 = ((bf16[64,8,3584]{2,1,0:T(8,128)(2,1)}), bf16[64,8,3584]{2,1,0:T(8,128)(2,1)}, u32[]{:S(2)}, u32[]{:S(2)}) async-start(bf16[64,8,3584]{2,1,0:T(8,128)(2,1)} %fusion.1), calls=%async_computation.3 | async-start | bytes 7340032 | tf_op jit(solution)/shard_map/all_to_all | solution.py:114
  349.4 0.0 copy-start.3
  349.5 2.7 convert_reduce_fusion.1
  352.1 0.6 fusion.7
  352.7 84.2 %all-to-all-done.3 = bf16[64,8,3584]{2,1,0:T(8,128)(2,1)} async-done(((bf16[64,8,3584]{2,1,0:T(8,128)(2,1)}), bf16[64,8,3584]{2,1,0:T(8,128)(2,1)}, u32[]{:S(2)}, u32[]{:S(2)}) %all-to-all-start.3) | async-done | bytes 3670048 | tf_op jit(solution)/shard_map/all_to_all | solution.py:114
  436.9 2.6 convert_reduce_fusion
  439.5 0.6 fusion.6
  440.1 11.0 %collective-permute-start = (bf16[2,24,3584]{2,1,0:T(8,128)(2,1)S(1)}, bf16[2,24,3584]{2,1,0:T(8,128)(2,1)S(1)}, u32[]{:S(2)}, u32[]{:S(2)}) collective-permute-start(bf16[2,24,3584]{2,1,0:T(8,128)(2,1)S(1)} %pad_maximum_fusion), channel_id=1, source_target_pairs={{0,448},{64,0},{128,64},{192,128},{256,192},{320,256},{384,320},{4... | collective-permute-start | bytes 1032200 | tf_op jit(solution)/shard_map/ppermute | solution.py:13
  451.2 22.4 %collective-permute-done = bf16[2,24,3584]{2,1,0:T(8,128)(2,1)S(1)} collective-permute-done((bf16[2,24,3584]{2,1,0:T(8,128)(2,1)S(1)}, bf16[2,24,3584]{2,1,0:T(8,128)(2,1)S(1)}, u32[]{:S(2)}, u32[]{:S(2)}) %collective-permute-start) | collective-permute-done | bytes 344096 | tf_op jit(solution)/shard_map/ppermute | solution.py:13
  473.6 0.7 fusion.52
  (11 shorter events, 0.1 us)
Async XLA Ops:
  0.6 124.7 %copy-start = (bf16[1,128,3584]{2,1,0:T(8,128)(2,1)S(1)}, bf16[1,128,3584]{2,1,0:T(8,128)(2,1)}, u32[]{:S(2)}) copy-start(bf16[1,128,3584]{2,1,0:T(8,128)(2,1)} %param.18) | copy-start | bytes 2752516
  6.8 15.6 %copy-start.6 = (s32[1,24,2]{1,2,0:T(2,128)S(1)}, s32[1,24,2]{1,2,0:T(2,128)}, u32[]{:S(2)}) copy-start(s32[1,24,2]{1,2,0:T(2,128)} %param.13) | copy-start | bytes 580
  6.8 16.4 %copy-start.7 = (f32[1,24,2]{1,2,0:T(2,128)S(1)}, f32[1,24,2]{1,2,0:T(2,128)}, u32[]{:S(2)}) copy-start(f32[1,24,2]{1,2,0:T(2,128)} %param.15) | copy-start | bytes 580
  6.8 16.5 %copy-start.4 = (bf16[1,24,3584]{2,1,0:T(8,128)(2,1)S(1)}, bf16[1,24,3584]{2,1,0:T(8,128)(2,1)}, u32[]{:S(2)}) copy-start(bf16[1,24,3584]{2,1,0:T(8,128)(2,1)} %param.11) | copy-start | bytes 516100
  6.9 100.2 %all-to-all-start = ((bf16[64,8,3584]{2,1,0:T(8,128)(2,1)}), bf16[64,8,3584]{2,1,0:T(8,128)(2,1)}, u32[]{:S(2)}, u32[]{:S(2)}) async-start(bf16[64,8,3584]{2,1,0:T(8,128)(2,1)} %bitcast.93), calls=%async_computation | async-start | bytes 7340032 | tf_op jit(solution)/shard_map/all_to_all | solution.py:76
  109.2 12.9 %copy-start.2 = (bf16[1,3584,128]{2,1,0:T(8,128)(2,1)S(1)}, bf16[1,3584,128]{2,1,0:T(8,128)(2,1)}, u32[]{:S(2)}) copy-start(bf16[1,3584,128]{2,1,0:T(8,128)(2,1)} %param.16) | copy-start | bytes 2752516
  109.2 108.2 %all-to-all-start.2 = ((bf16[64,8,3584]{2,1,0:T(8,128)(2,1)}), bf16[64,8,3584]{2,1,0:T(8,128)(2,1)}, u32[]{:S(2)}, u32[]{:S(2)}) async-start(bf16[64,8,3584]{2,1,0:T(8,128)(2,1)} %bitcast.94), calls=%async_computation.2 | async-start | bytes 7340032 | tf_op jit(solution)/shard_map/all_to_all | solution.py:77
  122.1 3.3 copy-start.1
  133.2 109.8 %copy-start.5 = (bf16[1,1,64,8,2,128]{5,4,3,2,1,0:T(2,128)(2,1)S(1)}, bf16[1,1,64,8,2,128]{5,4,3,2,1,0:T(2,128)(2,1)}, u32[]{:S(2)}) copy-start(bf16[1,1,64,8,2,128]{5,4,3,2,1,0:T(2,128)(2,1)} %param.19) | copy-start | bytes 786436
  217.4 115.5 %all-to-all-start.1 = ((bf16[64,8,3584]{2,1,0:T(8,128)(2,1)}), bf16[64,8,3584]{2,1,0:T(8,128)(2,1)}, u32[]{:S(2)}, u32[]{:S(2)}) async-start(bf16[64,8,3584]{2,1,0:T(8,128)(2,1)} %fusion), calls=%async_computation.1 | async-start | bytes 7340032 | tf_op jit(solution)/shard_map/all_to_all | solution.py:107
  332.9 104.0 %all-to-all-start.3 = ((bf16[64,8,3584]{2,1,0:T(8,128)(2,1)}), bf16[64,8,3584]{2,1,0:T(8,128)(2,1)}, u32[]{:S(2)}, u32[]{:S(2)}) async-start(bf16[64,8,3584]{2,1,0:T(8,128)(2,1)} %fusion.1), calls=%async_computation.3 | async-start | bytes 7340032 | tf_op jit(solution)/shard_map/all_to_all | solution.py:114
  349.4 2.7 copy-start.3
  440.1 33.5 %collective-permute-start = (bf16[2,24,3584]{2,1,0:T(8,128)(2,1)S(1)}, bf16[2,24,3584]{2,1,0:T(8,128)(2,1)S(1)}, u32[]{:S(2)}, u32[]{:S(2)}) collective-permute-start(bf16[2,24,3584]{2,1,0:T(8,128)(2,1)S(1)} %pad_maximum_fusion), channel_id=1, source_target_pairs={{0,448},{64,0},{128,64},{192,128},{256,192},{320,256},{384,320},{4... | collective-permute-start | bytes 1032200 | tf_op jit(solution)/shard_map/ppermute | solution.py:13
where the time goes:
time: 475 us; the launch traced here: 474 us
  waiting for transfers between devices  358 us (75%)
  starting transfers between devices  81.7 us (17%)
  matrix products  20.1 us (4%)
  other arithmetic  7.54 us (2%)
  local copies, waits for them, and re-layouts  6.51 us (1%)
    all_to_all x1, waiting for transfers between devices, on_device(): lax.all_to_all(widen(send_grads), 'ep', split_axis=0, concat_axis=0, tile...  84.3 us
    all_to_all x1, waiting for transfers between devices, on_device(): lax.all_to_all(grad_part.reshape(ep_size, capacity, width), 'ep', split_a...  84.2 us
    all_to_all x1, waiting for transfers between devices, on_device(): lax.all_to_all(out_part.reshape(ep_size, capacity, width), 'ep', split_ax...  83.6 us
    all_to_all x1, waiting for transfers between devices, on_device(): lax.all_to_all(widen(send_acts), 'ep', split_axis=0, concat_axis=0, tiled...  83.1 us
    all_to_all x1, starting transfers between devices, on_device(): lax.all_to_all(out_part.reshape(ep_size, capacity, width), 'ep', split_ax...  25.6 us
    ppermute x1, waiting for transfers between devices, from_behind(): return lax.ppermute(value, axis, pairs)  22.4 us
    all_to_all x1, starting transfers between devices, on_device(): lax.all_to_all(grad_part.reshape(ep_size, capacity, width), 'ep', split_a...  16.5 us
    all_to_all x1, starting transfers between devices, on_device(): lax.all_to_all(widen(send_acts), 'ep', split_axis=0, concat_axis=0, tiled...  15.6 us
  transfers between devices with their start and end apart: 5, of which 5 were waited for; matrix products, arithmetic and copies ran while one was open for 5% of the time, Pallas kernels for 0%

commit v1 on v0

v1 whole, which is shorter than its diff:
```python
import functools

import jax
import jax.numpy as jnp
from jax import lax
from jax.experimental import pallas as pl
from jax.experimental.pallas import tpu as pltpu
from jax.sharding import PartitionSpec as P

MESH = pl.DeviceIdType.MESH
BF = jnp.bfloat16
F32 = jnp.float32
TOK = 24
CAP = 8
PAIR = 16
NZ = 8
NY = 4
SLOTS = NZ * PAIR
TILE = 512
ORDER = (0, 1, 7, 2, 6, 3, 5, 4)
N_SEM = 208


def slot_table(routes, gates, shift, core):
    place = lax.broadcasted_iota(jnp.int32, (TOK, SLOTS), 1)
    expert = ((place >> 4) + shift) & 7
    mine = ((place >> 3) & 1) == core
    number = (place & 7).astype(F32)
    first = routes[:, 0:1] == expert
    second = routes[:, 1:2] == expert
    named = jnp.where(first | second, 1.0, 0.0).astype(BF)
    row = lax.broadcasted_iota(jnp.int32, (TOK, TOK), 0)
    col = lax.broadcasted_iota(jnp.int32, (TOK, TOK), 1)
    before = jnp.where(col < row, 1.0, 0.0).astype(BF)
    earlier = jnp.dot(before, named, preferred_element_type=F32)
    here = (earlier == number) & mine
    return jnp.where(here & first, gates[:, 0:1], 0.0) + jnp.where(here & second, gates[:, 1:2], 0.0)


def split(table):
    high = table.astype(BF)
    return high, (table - high.astype(F32)).astype(BF)


def plain(table):
    return jnp.where(table > 0.0, 1.0, 0.0).astype(BF)


def lead(a, b):
    return lax.dot_general(a, b, (((0,), (0,)), ((), ())), preferred_element_type=F32)


def trail(a, b):
    return lax.dot_general(a, b, (((1,), (1,)), ((), ())), preferred_element_type=F32)


def dot(a, b):
    return jnp.dot(a, b, preferred_element_type=F32)


def kernel(
    acts, grads, routes_f, routes_b, gates_f, gates_b, w_gate, w_up, w_down, stash,
    out_f, out_b,
    rows, part, back, slots, toks, tabs, sums, gets, wgu, wd, st, acc,
    send_sem, recv_sem, local_sem,
):
    width = rows.shape[2]
    tiles = width // TILE
    pp, ep = lax.axis_index("pp"), lax.axis_index("ep")
    n_pp = lax.axis_size("pp")
    z, y, core = ep // 8, lax.rem(ep, 8) // 2, lax.rem(ep, 2)
    pp_next = lax.rem(pp + n_pp - 1, n_pp)
    pp_prev = lax.rem(pp + 1, n_pp)

    def at_z(d):
        return lax.rem(z + d + NZ, NZ)

    def at_y(r):
        return lax.rem(y + r + NY, NY)

    def dev(d, r, c, section=None):
        return (pp if section is None else section, at_z(d) * 8 + at_y(r) * 2 + c)

    partner = dev(0, 0, 1 - core)

    ids, started, locals_ = {}, [], []

    def sem_of(key):
        return ids.setdefault(key, len(ids))

    def send(key, src, dst, target, lane=0):
        copy = pltpu.make_async_remote_copy(
            src_ref=src, dst_ref=dst, send_sem=send_sem.at[sem_of((key, lane) if lane else key)],
            recv_sem=recv_sem.at[sem_of(key)], device_id=target, device_id_type=MESH,
        )
        copy.start()
        started.append(copy)

    def arrive(key, dst):
        pltpu.make_async_remote_copy(
            src_ref=dst, dst_ref=dst, send_sem=send_sem.at[sem_of(key)],
            recv_sem=recv_sem.at[sem_of(key)], device_id=partner, device_id_type=MESH,
        ).wait_recv()

    def sent():
        for copy in started:
            copy.wait_send()
        started.clear()

    def local(src, dst):
        copy = pltpu.make_async_copy(src, dst, local_sem.at[len(locals_)])
        locals_.append(copy)
        copy.start()
        return copy

    def tiled(step):
        lax.fori_loop(0, tiles, lambda i, _: (step(pl.ds(pl.multiple_of(i * TILE, TILE), TILE)), 0)[1], 0)

    barrier = pltpu.get_barrier_semaphore()

    def greet(target):
        pl.semaphore_signal(barrier, inc=1, device_id=target, device_id_type=MESH)

    greet(partner)
    for d in range(1, NZ):
        greet(dev(d, 0, core))
    for r in (1, 3):
        greet(dev(0, r, core))
    greet(dev(0, 0, 0, pp_prev))
    for r in range(NY):
        greet(dev(0, r, 1, pp_prev))

    def load_weights(c):
        cols = pl.ds(c * 128, 128)
        ups = pl.ds((2 + c) * 128, 128)
        return [
            local(w_gate.at[0], wgu.at[:, cols]),
            local(w_up.at[0], wgu.at[:, ups]),
            local(w_down.at[0], wd.at[pl.ds(c * 128, 128)]),
        ]

    def send_weights(c):
        send(("gate", c), w_gate.at[0], wgu.at[:, pl.ds(c * 128, 128)], partner)
        send(("up", c), w_up.at[0], wgu.at[:, pl.ds((2 + c) * 128, 128)], partner)
        send(("down", c), w_down.at[0], wd.at[pl.ds(c * 128, 128)], partner)

    def get_weights(c):
        arrive(("gate", c), wgu.at[:, pl.ds(c * 128, 128)])
        arrive(("up", c), wgu.at[:, pl.ds((2 + c) * 128, 128)])
        arrive(("down", c), wd.at[pl.ds(c * 128, 128)])

    def build(base, r, tables, weighted):
        left = []
        for c in (0, 1):
            left.append(split(tables[c]) if weighted else (plain(tables[c]),))

        def step(cols):
            total = None
            for c in (0, 1):
                for one in left[c]:
                    term = lead(one, toks[r, c, :, cols])
                    total = term if total is None else total + term
            slots[pl.ds(base, NZ), :, cols] = total.astype(BF).reshape(NZ, PAIR, TILE)

        tiled(step)

    @pl.when(core == 0)
    def forward():
        near = local(acts.at[0], toks.at[0, 0])
        mine = load_weights(0)
        tabs[0, 0] = slot_table(routes_f[...], gates_f[...], z, 0)
        tabs[4, 0] = slot_table(routes_b[...], gates_b[...], 0, 0)
        pl.semaphore_wait(barrier, 12)
        send("grads", grads.at[0], toks.at[0, 0], partner)
        send("tab_b", tabs.at[4, 0], tabs.at[0, 0], partner)
        send("stash", stash, st.at[0], partner)
        send_weights(0)
        near.wait()
        arrive("acts", toks.at[0, 1])
        arrive("tab_f", tabs.at[0, 1])

        build(0, 0, (tabs[0, 0], tabs[0, 1]), False)

        def row(r, i):
            return (i // 4) * 16 + r * 4 + i % 4

        for i in range(1, NZ):
            d = ORDER[i]
            send(("zf", i), slots.at[d], rows.at[row(0, i)], dev(d, 0, 0))
        own = local(slots.at[0], rows.at[row(0, 0)])

        def spread(i):
            if i:
                arrive(("zf", i), rows.at[row(0, i)])
            source = rows.at[row(0, i)] if i else slots.at[0]
            send(("yp", i), source, rows.at[row(1, i)], dev(0, 1, 0))
            send(("ym", i), source, rows.at[row(3, i)], dev(0, 3, 0))

        def relay(i):
            arrive(("yp", i), rows.at[row(1, i)])
            arrive(("ym", i), rows.at[row(3, i)])
            if i % 2 == 0:
                send(("yy", i), rows.at[row(1, i)], rows.at[row(2, i)], dev(0, 1, 0))
            else:
                send(("yy", i), rows.at[row(3, i)], rows.at[row(2, i)], dev(0, 3, 0))

        def compute(h):
            for i in range(4 * h, 4 * h + 4):
                arrive(("yy", i), rows.at[row(2, i)])
            whole = pl.ds(16 * h, 16)
            acc[...] = jnp.zeros_like(acc)

            def one(cols):
                acc[...] += dot(rows[whole, :, cols].reshape(256, TILE), wgu[cols, :])

            tiled(one)
            gate, up = acc[:, :256], acc[:, 256:]
            hidden = (gate * jax.nn.sigmoid(gate) * up).astype(BF)

            def two(cols):
                part[whole, :, cols] = dot(hidden, wd[:, cols]).astype(BF).reshape(16, PAIR, TILE)

            tiled(two)

        def reduce_first(h):
            b = 16 * h
            q = 12 * h
            send(("rp", h), part.at[pl.ds(b + 8, 2)], back.at[pl.ds(q, 2)], dev(0, 1, 0))
            send(("rm", h), part.at[pl.ds(b + 10, 2)], back.at[pl.ds(q + 2, 2)], dev(0, 3, 0))
            send(("sp", h, 1), part.at[pl.ds(b + 14, 2)], back.at[pl.ds(q + 6, 2)], dev(0, 1, 0))
            send(("sm", h, 0), part.at[pl.ds(b + 4, 2)], back.at[pl.ds(q + 8, 2)], dev(0, 3, 0))

        def reduce_second(h):
            b = 16 * h
            q = 12 * h
            arrive(("rp", h), back.at[pl.ds(q, 2)])
            total = part[pl.ds(b + 12, 2)].astype(F32) + back[pl.ds(q, 2)].astype(F32)
            part[pl.ds(b + 12, 2)] = total.astype(BF)
            send(("sp", h, 0), part.at[pl.ds(b + 12, 2)], back.at[pl.ds(q + 4, 2)], dev(0, 1, 0))
            arrive(("rm", h), back.at[pl.ds(q + 2, 2)])
            total = part[pl.ds(b + 6, 2)].astype(F32) + back[pl.ds(q + 2, 2)].astype(F32)
            part[pl.ds(b + 6, 2)] = total.astype(BF)
            send(("sm", h, 1), part.at[pl.ds(b + 6, 2)], back.at[pl.ds(q + 10, 2)], dev(0, 3, 0))

        def reduce_last(h):
            b = 16 * h
            q = 12 * h
            arrive(("sp", h, 0), back.at[pl.ds(q + 4, 2)])
            arrive(("sp", h, 1), back.at[pl.ds(q + 6, 2)])
            arrive(("sm", h, 0), back.at[pl.ds(q + 8, 2)])
            arrive(("sm", h, 1), back.at[pl.ds(q + 10, 2)])
            for j in range(4):
                d = ORDER[4 * h + j]
                total = (
                    part[b + j].astype(F32) + back[q + 4 + j].astype(F32) + back[q + 8 + j].astype(F32)
                ).astype(BF)
                if d == 0:
                    back[24] = total
                else:
                    slots[8 + d] = total
                    send(("zr", d), slots.at[8 + d], back.at[24 + d], dev(-d, 0, 0))

        for i in range(4):
            spread(i)
            if i:
                relay(i - 1)
        relay(3)
        for i in range(4, 8):
            spread(i)
        own.wait()
        for copy in mine:
            copy.wait()
        get_weights(1)
        compute(0)
        for i in range(4, 8):
            relay(i)
        reduce_first(0)
        reduce_second(0)
        compute(1)
        reduce_first(1)
        reduce_last(0)
        reduce_second(1)
        reduce_last(1)
        for d in range(1, NZ):
            arrive(("zr", d), back.at[24 + d])
        for c in (0, 1):
            high, low = split(tabs[0, c])

            def step(cols):
                got = back[pl.ds(24, NZ), :, cols].reshape(SLOTS, TILE)
                total = toks[0, c, :, cols].astype(F32) + dot(high, got) + dot(low, got)
                sums[0, c, :, cols] = total.astype(BF)

            tiled(step)
            send(("out", 0), sums.at[0, c], out_f.at[0], dev(0, 0, c, pp_next), c)
        sent()

    locals_.clear()

    @pl.when(core == 1)
    def backward():
        mine = load_weights(1)
        near = local(grads.at[0], toks.at[0, 1])
        keep = local(stash, st.at[1])
        tabs[0, 1] = slot_table(routes_b[...], gates_b[...], 0, 1)
        tabs[4, 1] = slot_table(routes_f[...], gates_f[...], z, 1)
        pl.semaphore_wait(barrier, 18)
        send("acts", acts.at[0], toks.at[0, 1], partner)
        send("tab_f", tabs.at[4, 1], tabs.at[0, 1], partner)
        send(("tp", 1), grads.at[0], toks.at[1, 1], dev(0, 1, 1))
        send(("tm", 1), grads.at[0], toks.at[3, 1], dev(0, 3, 1))
        send_weights(1)
        arrive("grads", toks.at[0, 0])
        arrive("tab_b", tabs.at[0, 0])
        send(("tp", 0), toks.at[0, 0], toks.at[1, 0], dev(0, 1, 1))
        send(("tm", 0), toks.at[0, 0], toks.at[3, 0], dev(0, 3, 1))
        send("tabp", tabs.at[0], tabs.at[1], dev(0, 1, 1))
        send("tabm", tabs.at[0], tabs.at[2], dev(0, 3, 1))
        near.wait()
        own = []

        table_at = (0, 1, 3, 2)

        def scatter(r):
            build(8 * r, r, (tabs[table_at[r], 0], tabs[table_at[r], 1]), True)
            own.append(local(slots.at[8 * r + z], rows.at[8 * r + z]))
            for d in ORDER[1:]:
                send(("c", r, d), slots.at[8 * r + at_z(d)], rows.at[8 * r + z], dev(d, 0, 1))

        scatter(0)
        arrive(("tp", 0), toks.at[1, 0])
        arrive(("tp", 1), toks.at[1, 1])
        arrive("tabp", tabs.at[1])
        send(("ty", 0), toks.at[1, 0], toks.at[2, 0], dev(0, 1, 1))
        send("taby", tabs.at[1], tabs.at[3], dev(0, 1, 1))
        arrive(("tm", 0), toks.at[3, 0])
        arrive(("tm", 1), toks.at[3, 1])
        arrive("tabm", tabs.at[2])
        send(("ty", 1), toks.at[3, 1], toks.at[2, 1], dev(0, 3, 1))
        scatter(1)
        scatter(3)
        arrive(("ty", 0), toks.at[2, 0])
        arrive(("ty", 1), toks.at[2, 1])
        arrive("taby", tabs.at[3])
        scatter(2)

        for copy in mine:
            copy.wait()
        keep.wait()
        get_weights(0)
        arrive("stash", st.at[0])
        pick_row = lax.broadcasted_iota(jnp.int32, (SLOTS, 2 * SLOTS), 0)
        pick_col = lax.broadcasted_iota(jnp.int32, (SLOTS, 2 * SLOTS), 1)
        even = jnp.where(pick_col == 2 * pick_row, 1.0, 0.0).astype(BF)
        odd = jnp.where(pick_col == 2 * pick_row + 1, 1.0, 0.0).astype(BF)

        def compute(r, own_copy):
            own_copy.wait()
            for d in ORDER[1:]:
                arrive(("c", r, d), rows.at[8 * r + at_z(-d)])
            whole = pl.ds(8 * r, NZ)
            acc[0:SLOTS, 0:256] = jnp.zeros((SLOTS, 256), F32)

            def one(cols):
                acc[0:SLOTS, 0:256] += trail(rows[whole, :, cols].reshape(SLOTS, TILE), wd[:, cols])

            tiled(one)
            grad = []
            for c in (0, 1):
                both = st[c, :, at_y(-r)].reshape(2 * SLOTS, 128)
                gate, up = dot(even, both), dot(odd, both)
                q = jax.nn.sigmoid(gate)
                hidden = acc[0:SLOTS, 128 * c : 128 * c + 128]
                grad.append(
                    (
                        (hidden * up * q * (1.0 + gate * (1.0 - q))).astype(BF),
                        (hidden * gate * q).astype(BF),
                    )
                )
            both = jnp.concatenate([grad[0][0], grad[1][0], grad[0][1], grad[1][1]], axis=1)

            def two(cols):
                part[whole, :, cols] = trail(both, wgu[cols, :]).astype(BF).reshape(NZ, PAIR, TILE)

            tiled(two)
            own.append(local(part.at[8 * r + z], back.at[8 * r + z]))
            for d in ORDER[1:]:
                send(("p", r, d), part.at[8 * r + at_z(-d)], back.at[8 * r + z], dev(-d, 0, 1))

        def combine(r, own_copy):
            own_copy.wait()
            for d in ORDER[1:]:
                arrive(("p", r, d), back.at[8 * r + at_z(d)])
            for c in (0, 1):
                table = plain(tabs[table_at[r], c])

                def step(cols):
                    total = dot(table, back[pl.ds(8 * r, NZ), :, cols].reshape(SLOTS, TILE))
                    if r == 0:
                        total = total + toks[0, c, :, cols].astype(F32)
                    sums[r, c, :, cols] = total.astype(BF)

                tiled(step)
                send(("end", r), sums.at[r, c], gets.at[r], dev(0, -r, c, pp_next), c)

        order = (0, 1, 3, 2)
        for n, r in enumerate(order):
            compute(r, own[n])
        for n, r in enumerate(order):
            combine(r, own[4 + n])
        sent()

    for r in (0, 1, 3, 2):
        arrive(("end", r), gets.at[r])

    def total(cols):
        out_b[0, :, cols] = (
            gets[0, :, cols].astype(F32)
            + gets[1, :, cols].astype(F32)
            + gets[2, :, cols].astype(F32)
            + gets[3, :, cols].astype(F32)
        ).astype(BF)

    tiled(total)
    arrive(("out", 0), out_f.at[0])
    assert len(ids) <= N_SEM


def on_device(acts, grads, routes_f, routes_b, gates_f, gates_b, w_gate, w_up, w_down, stash):
    width = acts.shape[2]
    anywhere = pl.BlockSpec(memory_space=pl.ANY)
    inside = pl.BlockSpec(memory_space=pltpu.VMEM)
    out = jax.ShapeDtypeStruct((1, TOK, width), BF)
    chunks = pltpu.VMEM((NZ * NY, PAIR, width), BF)
    return pl.pallas_call(
        kernel,
        name="relay",
        out_shape=(out, out),
        in_specs=[anywhere, anywhere, inside, inside, inside, inside] + [anywhere] * 4,
        out_specs=(anywhere, inside),
        scratch_shapes=[
            chunks,
            chunks,
            chunks,
            chunks,
            pltpu.VMEM((NY, 2, TOK, width), BF),
            pltpu.VMEM((5, 2, TOK, SLOTS), F32),
            pltpu.VMEM((NY, 2, TOK, width), BF),
            pltpu.VMEM((NY, TOK, width), BF),
            pltpu.VMEM((width, 512), BF),
            pltpu.VMEM((256, width), BF),
            pltpu.VMEM((2, NZ, NY, 32, 128), BF),
            pltpu.VMEM((256, 512), F32),
            pltpu.SemaphoreType.DMA((N_SEM,)),
            pltpu.SemaphoreType.DMA((N_SEM,)),
            pltpu.SemaphoreType.DMA((16,)),
        ],
        compiler_params=pltpu.CompilerParams(
            collective_id=0, has_side_effects=True, vmem_limit_bytes=56 * 2**20
        ),
    )(
        acts, grads, routes_f[0], routes_b[0], gates_f[0], gates_b[0],
        w_gate, w_up, w_down, stash.reshape(NZ, NY, 32, 128),
    )


def solution(mesh):
    placed = (
        P("pp", "ep", None),
        P("pp", "ep", None),
        P("pp", "ep", None),
        P("pp", "ep", None),
        P("pp", "ep", None),
        P("pp", "ep", None),
        P("pp", None, "ep"),
        P("pp", None, "ep"),
        P("pp", "ep", None),
        P("pp", "ep", None, None, None, None),
    )
    return jax.shard_map(
        on_device,
        mesh=mesh,
        in_specs=placed,
        out_specs=(P("pp", "ep", None), P("pp", "ep", None)),
        check_vma=False,
    )
```

time: 475 us -> 141 us (0.30)
  the two profiles are of different devices: /device:TPU:104 before, /device:TPU:59 now
where the time goes in v1:
time: 141 us; the launch traced here: 140 us
  Pallas kernels  134 us (95%)
  local copies, waits for them, and re-layouts  5.72 us (4%)
    pallas_call x1, Pallas kernels, on_device(): pl.pallas_call(kernel, name='relay', out_shape=(out, out), in_specs=[anyw...  134 us
    unnamed x12, local copies, waits for them, and re-layouts  2.99 us

profile of v1, /device:TPU:59, one launch (start us, length us, event | category | flops | bytes accessed | tf_op | source)
XLA Modules:
  0.0 140.3 jit_solution(2690968511496757331)
XLA Ops:
  0.6 0.0 copy-start.1
  0.6 0.7 copy-done.1
  1.3 0.0 copy-start.2
  1.3 0.7 copy.12.routes_f
  2.0 0.0 copy-done.2
  2.0 0.0 copy-start.3
  2.0 0.7 copy.13.routes_b
  2.7 0.0 copy-done.3
  2.7 0.0 copy-start.4
  2.7 0.7 copy.14.gates_f
  3.4 0.0 copy-done.4
  3.4 0.7 copy.15.gates_b
  4.1 133.9 %relay.1 = (bf16[1,24,3584]{2,1,0:T(8,128)(2,1)}, bf16[1,24,3584]{2,1,0:T(8,128)(2,1)}) custom-call(bf16[1,24,3584]{2,1,0:T(8,128)(2,1)} %acts.1, bf16[1,24,3584]{2,1,0:T(8,128)(2,1)} %grads.1, s32[24,2]{1,0:T(8,128)} %copy.12.routes_f, s32[24,2]{1,0:T(8,128)} %copy.13.routes_b, f32[24,2]{1,0:T(8,128)} %copy.14.gates_f, f32[24,2]{1,0:T(8,128)} %copy.15.gates_b, ...), custom_call_target="tpu_custom_call" | custom-call | tf_op jit(solution)/shard_map/relay/pallas_call | solution.py:435
  138.0 0.0 copy-start
  138.0 1.6 %copy.18 = bf16[1,24,3584]{2,1,0:T(8,128)(2,1)} copy(bf16[1,24,3584]{2,1,0:T(8,128)(2,1)} %get-tuple-element.4) | data formatting | bytes 344064
  139.6 0.0 copy-done
  139.7 0.7 copy.19
Async XLA Ops:
  0.6 0.7 copy-start.1
  1.3 0.7 copy-start.2
  2.0 0.7 copy-start.3
  2.7 0.7 copy-start.4
  138.0 1.6 %copy-start = (bf16[1,24,3584]{2,1,0:T(8,128)(2,1)S(1)}, bf16[1,24,3584]{2,1,0:T(8,128)(2,1)}, u32[]{:S(2)}) copy-start(bf16[1,24,3584]{2,1,0:T(8,128)(2,1)} %get-tuple-element.5) | copy-start | bytes 516100

commit v2 on v1

v2 whole, which is shorter than its diff:
```python
import functools

import jax
import jax.numpy as jnp
from jax import lax
from jax.experimental import pallas as pl
from jax.experimental.pallas import tpu as pltpu
from jax.sharding import PartitionSpec as P

MESH = pl.DeviceIdType.MESH
BF = jnp.bfloat16
F32 = jnp.float32
TOK = 24
CAP = 8
PAIR = 16
NZ = 8
NY = 4
SLOTS = NZ * PAIR
TILE = 512
ORDER = (0, 1, 7, 2, 6, 3, 5, 4)
CLOSE = ORDER[1:7]
APART = ORDER[7:]
LAG = 2
GATE = 3
FLOW = ("mid", "near", "far", "own")
N_SEM = 208


def slot_table(routes, gates, shift, core):
    place = lax.broadcasted_iota(jnp.int32, (SLOTS, TOK), 0)
    expert = ((place >> 4) + shift) & 7
    mine = ((place >> 3) & 1) == core
    number = (place & 7).astype(F32)
    first = routes[0:1, :] == expert
    second = routes[1:2, :] == expert
    named = jnp.where(first | second, 1.0, 0.0).astype(BF)
    row = lax.broadcasted_iota(jnp.int32, (TOK, TOK), 0)
    col = lax.broadcasted_iota(jnp.int32, (TOK, TOK), 1)
    before = jnp.where(row < col, 1.0, 0.0).astype(BF)
    earlier = dot(named, before)
    here = (earlier == number) & mine
    return jnp.where(here & first, gates[0:1, :], 0.0) + jnp.where(here & second, gates[1:2, :], 0.0)


def split(table):
    high = table.astype(BF)
    return high, (table - high.astype(F32)).astype(BF)


def plain(table):
    return jnp.where(table > 0.0, 1.0, 0.0).astype(BF)


def lead(a, b):
    return lax.dot_general(a, b, (((0,), (0,)), ((), ())), preferred_element_type=F32)


def trail(a, b):
    return lax.dot_general(a, b, (((1,), (1,)), ((), ())), preferred_element_type=F32)


def dot(a, b):
    return jnp.dot(a, b, preferred_element_type=F32)


def kernel(
    acts, grads, routes_f, routes_b, gates_f, gates_b, w_gate, w_up, w_down, stash,
    out_f, out_b,
    rows, part, back, slots, toks, named, scale, sums, gets, wgu, wd, st, acc,
    send_sem, recv_sem, local_sem, go,
):
    width = rows.shape[2]
    tiles = width // TILE
    pp, ep = lax.axis_index("pp"), lax.axis_index("ep")
    n_pp = lax.axis_size("pp")
    z, y, core = ep // 8, lax.rem(ep, 8) // 2, lax.rem(ep, 2)
    pp_next = lax.rem(pp + n_pp - 1, n_pp)
    pp_prev = lax.rem(pp + 1, n_pp)
    side = 2 * lax.rem(pp, 2) - 1
    mid, near = 2 - side, 2 + side

    def at_z(d):
        return lax.rem(z + d + NZ, NZ)

    def at_y(r):
        return lax.rem(y + r + NY, NY)

    def dev(d, r, c, section=None):
        return (pp if section is None else section, at_z(d) * 8 + at_y(r) * 2 + c)

    partner = dev(0, 0, 1 - core)

    ids, started, locals_ = {}, [], []

    def sem_of(key):
        return ids.setdefault(key, len(ids))

    def send(key, src, dst, target, lane=0):
        copy = pltpu.make_async_remote_copy(
            src_ref=src, dst_ref=dst, send_sem=send_sem.at[sem_of((key, lane) if lane else key)],
            recv_sem=recv_sem.at[sem_of(key)], device_id=target, device_id_type=MESH,
        )
        copy.start()
        started.append(copy)

    def arrive(key, dst):
        pltpu.make_async_remote_copy(
            src_ref=dst, dst_ref=dst, send_sem=send_sem.at[sem_of(key)],
            recv_sem=recv_sem.at[sem_of(key)], device_id=partner, device_id_type=MESH,
        ).wait_recv()

    def sent():
        for copy in started:
            copy.wait_send()
        started.clear()

    def local(src, dst):
        copy = pltpu.make_async_copy(src, dst, local_sem.at[len(locals_)])
        locals_.append(copy)
        copy.start()
        return copy

    def tiled(step):
        lax.fori_loop(0, tiles, lambda i, _: (step(pl.ds(pl.multiple_of(i * TILE, TILE), TILE)), 0)[1], 0)

    barrier = pltpu.get_barrier_semaphore()

    def greet(target):
        pl.semaphore_signal(barrier, inc=1, device_id=target, device_id_type=MESH)

    greet(partner)
    for d in range(1, NZ):
        greet(dev(d, 0, core))
    for r in (1, 3):
        greet(dev(0, r, core))
    greet(dev(0, 0, 1, pp_prev))
    greet(dev(0, side, 1, pp_prev))

    @pl.when(core == 0)
    def others():
        greet(dev(0, 0, 0, pp_prev))
        greet(dev(0, side, 0, pp_prev))

    @pl.when(core == 1)
    def across():
        greet(dev(0, 2, 1))

    def load_weights(c):
        cols = pl.ds(c * 128, 128)
        ups = pl.ds((2 + c) * 128, 128)
        return [
            local(w_gate.at[0], wgu.at[:, cols]),
            local(w_up.at[0], wgu.at[:, ups]),
            local(w_down.at[0], wd.at[pl.ds(c * 128, 128)]),
        ]

    def send_weights(c):
        send(("gate", c), w_gate.at[0], wgu.at[:, pl.ds(c * 128, 128)], partner)
        send(("up", c), w_up.at[0], wgu.at[:, pl.ds((2 + c) * 128, 128)], partner)
        send(("down", c), w_down.at[0], wd.at[pl.ds(c * 128, 128)], partner)

    def get_weights(c):
        arrive(("gate", c), wgu.at[:, pl.ds(c * 128, 128)])
        arrive(("up", c), wgu.at[:, pl.ds((2 + c) * 128, 128)])
        arrive(("down", c), wd.at[pl.ds(c * 128, 128)])

    def build(base, r, tables, weighted):
        left = []
        for c in (0, 1):
            left.append(split(tables[c]) if weighted else (plain(tables[c]),))

        def step(cols):
            total = None
            for c in (0, 1):
                for one in left[c]:
                    term = dot(one, toks[r, c, :, cols])
                    total = term if total is None else total + term
            slots[pl.ds(base, NZ), :, cols] = total.astype(BF).reshape(NZ, PAIR, TILE)

        tiled(step)

    @pl.when(core == 0)
    def forward():
        waits = [
            local(acts.at[0], toks.at[0, 0]),
            local(routes_f, named.at[0, 0]),
            local(gates_f, scale.at[0, 0]),
        ]
        mine = load_weights(0)
        pl.semaphore_wait(barrier, 12)
        send("routes_b", routes_b, named.at[0, 0], partner)
        send("gates_b", gates_b, scale.at[0, 0], partner)
        send("grads", grads.at[0], toks.at[0, 0], partner)
        send(("nextn", 0), routes_f, named.at[1, 0], dev(0, 0, 0, pp_next))
        send(("nexts", 0), gates_f, scale.at[1, 0], dev(0, 0, 0, pp_next))
        for copy in waits:
            copy.wait()
        arrive("routes_f", named.at[0, 1])
        arrive("gates_f", scale.at[0, 1])
        tables = [slot_table(named[0, c], scale[0, c], z, c) for c in (0, 1)]
        arrive("acts", toks.at[0, 1])

        build(0, 0, tables, False)

        def row(r, i):
            return (i // 4) * 16 + r * 4 + i % 4

        for i in range(1, NZ):
            d = ORDER[i]
            send(("zf", i), slots.at[d], rows.at[row(0, i)], dev(d, 0, 0))
        own = local(slots.at[0], rows.at[row(0, 0)])

        def spread(i):
            if i:
                arrive(("zf", i), rows.at[row(0, i)])
            if i == GATE:
                pl.semaphore_signal(go, inc=1, device_id=partner, device_id_type=MESH)
            source = rows.at[row(0, i)] if i else slots.at[0]
            send(("yp", i), source, rows.at[row(1, i)], dev(0, 1, 0))
            send(("ym", i), source, rows.at[row(3, i)], dev(0, 3, 0))

        def relay(i):
            arrive(("yp", i), rows.at[row(1, i)])
            arrive(("ym", i), rows.at[row(3, i)])
            if i % 2 == 0:
                send(("yy", i), rows.at[row(1, i)], rows.at[row(2, i)], dev(0, 1, 0))
            else:
                send(("yy", i), rows.at[row(3, i)], rows.at[row(2, i)], dev(0, 3, 0))

        def compute(h):
            for i in range(4 * h, 4 * h + 4):
                arrive(("yy", i), rows.at[row(2, i)])
            whole = pl.ds(16 * h, 16)
            acc[...] = jnp.zeros_like(acc)

            def one(cols):
                acc[...] += dot(rows[whole, :, cols].reshape(256, TILE), wgu[cols, :])

            tiled(one)
            gate, up = acc[:, :256], acc[:, 256:]
            hidden = (gate * jax.nn.sigmoid(gate) * up).astype(BF)

            def two(cols):
                part[whole, :, cols] = dot(hidden, wd[:, cols]).astype(BF).reshape(16, PAIR, TILE)

            tiled(two)

        def spot(g, r):
            return pl.ds(16 * (g // 2) + 2 * (g % 2) + 4 * r, 2)

        def land(g, n):
            return pl.ds(8 * g + 2 * n, 2)

        def reduce_first(g):
            send(("r2", g), part.at[spot(g, 2)], back.at[land(g, 0)], dev(0, side, 0))
            send(("rm", g), part.at[spot(g, mid)], back.at[land(g, 1)], dev(0, -side, 0))

        def reduce_second(g):
            for name, n, r, target in (("r2", 0, near, side), ("rm", 1, 0, 0)):
                arrive((name, g), back.at[land(g, n)])

                def add(cols):
                    total = part[spot(g, r), :, cols].astype(F32) + back[land(g, n), :, cols].astype(F32)
                    part[spot(g, r), :, cols] = total.astype(BF)

                tiled(add)
                send(("s" + name, g), part.at[spot(g, r)], back.at[land(g, 2 + n)], dev(0, target, 0, pp_next))

        def reduce_last(g):
            arrive(("sr2", g), back.at[land(g, 2)])
            arrive(("srm", g), back.at[land(g, 3)])
            for j in (1, 0):
                d = ORDER[2 * g + j]
                place = 16 if d == 0 else 8 + d

                def add(cols):
                    total = back[8 * g + 4 + j, :, cols].astype(F32) + back[8 * g + 6 + j, :, cols].astype(F32)
                    slots[place, :, cols] = total.astype(BF)

                tiled(add)
                if d:
                    send(("zr", d), slots.at[8 + d], slots.at[16 + d], dev(-d, 0, 0))

        for i in range(LAG):
            spread(i)
        send("stash", stash, st.at[0], partner)
        send_weights(0)
        for i in range(4):
            spread(i + LAG)
            relay(i)
        for i in range(4 + LAG, NZ):
            spread(i)
        send(("next", 0), acts.at[0], toks.at[1, 0], dev(0, 0, 0, pp_next))
        own.wait()
        for copy in mine:
            copy.wait()
        get_weights(1)
        compute(0)
        for i in range(4, 8):
            relay(i)
        reduce_first(0)
        reduce_first(1)
        compute(1)
        reduce_second(0)
        reduce_second(1)
        reduce_first(2)
        reduce_first(3)
        reduce_last(0)
        reduce_second(2)
        reduce_last(1)
        reduce_second(3)
        reduce_last(2)
        reduce_last(3)
        for c in (0, 1):
            arrive(("next", c), toks.at[1, c])
            arrive(("nextn", c), named.at[1, c])
            arrive(("nexts", c), scale.at[1, c])
        left = [split(slot_table(named[1, c], scale[1, c], z, c)) for c in (0, 1)]
        for d in range(1, NZ):
            arrive(("zr", d), slots.at[16 + d])
        for c in (1, 0):
            high, low = left[c]

            def step(cols):
                got = slots[pl.ds(16, NZ), :, cols].reshape(SLOTS, TILE)
                total = toks[1, c, :, cols].astype(F32) + lead(high, got) + lead(low, got)
                sums[0, c, :, cols] = total.astype(BF)

            tiled(step)
            if c:
                send("out", sums.at[0, 1], out_f.at[0], partner)
            else:
                last = local(sums.at[0, 0], out_f.at[0])
        last.wait()
        sent()

    locals_.clear()

    @pl.when(core == 1)
    def backward():
        waits = [
            local(grads.at[0], toks.at[0, 1]),
            local(routes_b, named.at[0, 1]),
            local(gates_b, scale.at[0, 1]),
        ]
        keep = local(stash, st.at[1])
        mine = load_weights(1)
        pl.semaphore_wait(barrier, 15)
        send("routes_f", routes_f, named.at[0, 1], partner)
        send("gates_f", gates_f, scale.at[0, 1], partner)
        send("acts", acts.at[0], toks.at[0, 1], partner)
        send(("tm", 1), grads.at[0], toks.at[mid, 1], dev(0, side, 1))
        send(("tn", 1), grads.at[0], toks.at[near, 1], dev(0, -side, 1))
        for copy in waits:
            copy.wait()
        arrive("routes_b", named.at[0, 0])
        arrive("gates_b", scale.at[0, 0])
        for name, r, target in (("mid", mid, side), ("near", near, -side), ("far", 2, 2)):
            send(("nr", name), named.at[0], named.at[r], dev(0, target, 1))
            send(("ng", name), scale.at[0], scale.at[r], dev(0, target, 1))
        arrive("grads", toks.at[0, 0])
        send(("tm", 0), toks.at[0, 0], toks.at[mid, 0], dev(0, side, 1))
        send(("tn", 0), toks.at[0, 0], toks.at[near, 0], dev(0, -side, 1))
        own = {}
        index = {"own": 0, "mid": mid, "near": near, "far": 2}

        def tables(r):
            return [slot_table(named[r, c], scale[r, c], 0, c) for c in (0, 1)]

        def scatter(name):
            r = index[name]
            if name != "own":
                arrive(("nr", name), named.at[r])
                arrive(("ng", name), scale.at[r])
            build(8 * r, r, tables(r), True)
            own[name] = local(slots.at[8 * r + z], rows.at[8 * r + z])
            if name == "own" and GATE >= 0:
                pl.semaphore_wait(go, 1)
            for d in (APART + CLOSE if name == "own" else CLOSE):
                send(("c", name, d), slots.at[8 * r + at_z(d)], rows.at[8 * r + z], dev(d, 0, 1))

        scatter("own")
        send_weights(1)
        arrive(("tm", 0), toks.at[mid, 0])
        arrive(("tm", 1), toks.at[mid, 1])
        send(("ty", 0), toks.at[mid, 0], toks.at[2, 0], dev(0, side, 1))
        arrive(("tn", 0), toks.at[near, 0])
        arrive(("tn", 1), toks.at[near, 1])
        send(("ty", 1), toks.at[near, 1], toks.at[2, 1], dev(0, -side, 1))
        send(("next", 1), acts.at[0], toks.at[1, 1], dev(0, 0, 0, pp_next))
        send(("nextn", 1), routes_f, named.at[1, 1], dev(0, 0, 0, pp_next))
        send(("nexts", 1), gates_f, scale.at[1, 1], dev(0, 0, 0, pp_next))
        scatter("mid")
        scatter("near")
        arrive(("ty", 0), toks.at[2, 0])
        arrive(("ty", 1), toks.at[2, 1])
        scatter("far")

        half = pl.ds(0, width // 2)
        rest = pl.ds(width // 2, width // 2)
        for d in APART:
            source = at_z(-d)
            arrive(("c", "own", d), rows.at[source])
            send(("fp", d), rows.at[source], rows.at[8 * mid + source], dev(0, side, 1))
            send(("fm", d), rows.at[source], rows.at[8 * near + source], dev(0, -side, 1))
        for d in APART:
            source = at_z(-d)
            arrive(("fp", d), rows.at[8 * mid + source])
            send(("fy", 0, d), rows.at[8 * mid + source, :, half], rows.at[16 + source, :, half], dev(0, side, 1))
            arrive(("fm", d), rows.at[8 * near + source])
            send(("fy", 1, d), rows.at[8 * near + source, :, rest], rows.at[16 + source, :, rest], dev(0, -side, 1))

        for copy in mine:
            copy.wait()
        keep.wait()
        get_weights(0)
        arrive("stash", st.at[0])
        pick_row = lax.broadcasted_iota(jnp.int32, (SLOTS, 2 * SLOTS), 0)
        pick_col = lax.broadcasted_iota(jnp.int32, (SLOTS, 2 * SLOTS), 1)
        even = jnp.where(pick_col == 2 * pick_row, 1.0, 0.0).astype(BF)
        odd = jnp.where(pick_col == 2 * pick_row + 1, 1.0, 0.0).astype(BF)

        def compute(name):
            r = index[name]
            own[name].wait()
            for d in CLOSE:
                arrive(("c", name, d), rows.at[8 * r + at_z(-d)])
            if name == "far":
                for d in APART:
                    arrive(("fy", 0, d), rows.at[16 + at_z(-d), :, half])
                    arrive(("fy", 1, d), rows.at[16 + at_z(-d), :, rest])
            whole = pl.ds(8 * r, NZ)
            acc[0:SLOTS, 0:256] = jnp.zeros((SLOTS, 256), F32)

            def one(cols):
                acc[0:SLOTS, 0:256] += trail(rows[whole, :, cols].reshape(SLOTS, TILE), wd[:, cols])

            tiled(one)
            grad = []
            for c in (0, 1):
                both = st[c, :, at_y(-r)].reshape(2 * SLOTS, 128)
                gate, up = dot(even, both), dot(odd, both)
                q = jax.nn.sigmoid(gate)
                hidden = acc[0:SLOTS, 128 * c : 128 * c + 128]
                grad.append(
                    (
                        (hidden * up * q * (1.0 + gate * (1.0 - q))).astype(BF),
                        (hidden * gate * q).astype(BF),
                    )
                )
            both = jnp.concatenate([grad[0][0], grad[1][0], grad[0][1], grad[1][1]], axis=1)

            def two(cols):
                part[whole, :, cols] = trail(both, wgu[cols, :]).astype(BF).reshape(NZ, PAIR, TILE)

            tiled(two)
            own[name] = local(part.at[8 * r + z], back.at[8 * r + z])
            for d in ORDER[1:]:
                send(("p", name, d), part.at[8 * r + at_z(-d)], back.at[8 * r + z], dev(-d, 0, 1))

        def combine(name):
            r = index[name]
            own[name].wait()
            for d in ORDER[1:]:
                arrive(("p", name, d), back.at[8 * r + at_z(d)])
            for c, table in enumerate(tables(r)):
                table = plain(table)
                if name == "near":
                    arrive(("e1", c), gets.at[2 + c])
                if name == "own":
                    arrive(("e2", c), gets.at[4 + c])

                def step(cols):
                    total = lead(table, back[pl.ds(8 * r, NZ), :, cols].reshape(SLOTS, TILE))
                    if name == "near":
                        total = total + gets[2 + c, :, cols].astype(F32)
                    if name == "own":
                        total = total + gets[4 + c, :, cols].astype(F32) + toks[0, c, :, cols].astype(F32)
                    sums[r, c, :, cols] = total.astype(BF)

                tiled(step)
                if name == "far":
                    send(("e1", c), sums.at[r, c], gets.at[2 + c], dev(0, side, 1))
                if name == "mid":
                    send(("e2", c), sums.at[r, c], gets.at[4 + c], dev(0, -side, 1))
                if name == "near":
                    send("end1", sums.at[r, c], gets.at[1], dev(0, side, c, pp_next), c)
                if name == "own":
                    send("end0", sums.at[r, c], gets.at[0], dev(0, 0, c, pp_next), c)

        order = ("far", "mid", "near", "own")
        for name in FLOW:
            compute(name)
        for name in order:
            combine(name)
        arrive("out", out_f.at[0])
        sent()

    arrive("end1", gets.at[1])
    arrive("end0", gets.at[0])

    def total(cols):
        out_b[0, :, cols] = (gets[0, :, cols].astype(F32) + gets[1, :, cols].astype(F32)).astype(BF)

    tiled(total)
    assert len(ids) <= N_SEM


def on_device(acts, grads, routes_f, routes_b, gates_f, gates_b, w_gate, w_up, w_down, stash):
    width = acts.shape[2]
    anywhere = pl.BlockSpec(memory_space=pl.ANY)
    inside = pl.BlockSpec(memory_space=pltpu.VMEM)
    out = jax.ShapeDtypeStruct((1, TOK, width), BF)
    chunks = pltpu.VMEM((NZ * NY, PAIR, width), BF)
    return pl.pallas_call(
        kernel,
        name="relay",
        out_shape=(out, out),
        in_specs=[anywhere] * 10,
        out_specs=(anywhere, inside),
        scratch_shapes=[
            chunks,
            chunks,
            chunks,
            chunks,
            pltpu.VMEM((NY, 2, TOK, width), BF),
            pltpu.VMEM((NY, 2, 2, TOK), jnp.int32),
            pltpu.VMEM((NY, 2, 2, TOK), F32),
            pltpu.VMEM((NY, 2, TOK, width), BF),
            pltpu.VMEM((6, TOK, width), BF),
            pltpu.VMEM((width, 512), BF),
            pltpu.VMEM((256, width), BF),
            pltpu.VMEM((2, NZ, NY, 32, 128), BF),
            pltpu.VMEM((256, 512), F32),
            pltpu.SemaphoreType.DMA((N_SEM,)),
            pltpu.SemaphoreType.DMA((N_SEM,)),
            pltpu.SemaphoreType.DMA((16,)),
            pltpu.SemaphoreType.REGULAR,
        ],
        compiler_params=pltpu.CompilerParams(
            collective_id=0, has_side_effects=True, vmem_limit_bytes=56 * 2**20
        ),
    )(
        acts, grads, routes_f[0].T, routes_b[0].T, gates_f[0].T, gates_b[0].T,
        w_gate, w_up, w_down, stash.reshape(NZ, NY, 32, 128),
    )


def solution(mesh):
    placed = (
        P("pp", "ep", None),
        P("pp", "ep", None),
        P("pp", "ep", None),
        P("pp", "ep", None),
        P("pp", "ep", None),
        P("pp", "ep", None),
        P("pp", None, "ep"),
        P("pp", None, "ep"),
        P("pp", "ep", None),
        P("pp", "ep", None, None, None, None),
    )
    return jax.shard_map(
        on_device,
        mesh=mesh,
        in_specs=placed,
        out_specs=(P("pp", "ep", None), P("pp", "ep", None)),
        check_vma=False,
    )
```

time: 141 us -> 128 us (0.908)
  the two profiles are of different devices: /device:TPU:59 before, /device:TPU:12 now
where the time goes in v2:
time: 128 us
  Pallas kernels  125 us (98%)
  local copies, waits for them, and re-layouts  2.31 us (2%)
    pallas_call x1, Pallas kernels, on_device(): pl.pallas_call(kernel, name='relay', out_shape=(out, out), in_specs=[anyw...  125 us

profile of v2, /device:TPU:12, one launch (start us, length us, event | category | flops | bytes accessed | tf_op | source)
XLA Modules:
  0.0 127.7 jit_solution(17491278318629768006)
XLA Ops:
  0.6 124.8 %relay.1 = (bf16[1,24,3584]{2,1,0:T(8,128)(2,1)}, bf16[1,24,3584]{2,1,0:T(8,128)(2,1)}) custom-call(bf16[1,24,3584]{2,1,0:T(8,128)(2,1)} %acts.1, bf16[1,24,3584]{2,1,0:T(8,128)(2,1)} %grads.1, s32[2,24]{1,0:T(2,128)} %bitcast.14, s32[2,24]{1,0:T(2,128)} %bitcast.15, f32[2,24]{1,0:T(2,128)} %bitcast.16, f32[2,24]{1,0:T(2,128)} %bitcast.17, ...), custom_call_target="tpu_custom_call" | custom-call | tf_op jit(solution)/shard_map/relay/pallas_call | solution.py:515
  125.4 0.0 copy-start
  125.4 1.6 %copy.14 = bf16[1,24,3584]{2,1,0:T(8,128)(2,1)} copy(bf16[1,24,3584]{2,1,0:T(8,128)(2,1)} %get-tuple-element.4) | data formatting | bytes 344064
  127.1 0.0 copy-done
  127.1 0.7 copy.15
Async XLA Ops:
  125.4 1.6 %copy-start = (bf16[1,24,3584]{2,1,0:T(8,128)(2,1)S(1)}, bf16[1,24,3584]{2,1,0:T(8,128)(2,1)}, u32[]{:S(2)}) copy-start(bf16[1,24,3584]{2,1,0:T(8,128)(2,1)} %get-tuple-element.5) | copy-start | bytes 516100

commit v3 on v2

--- a/solution.py
+++ b/solution.py
@@ -21,7 +21,7 @@
 CLOSE = ORDER[1:7]
 APART = ORDER[7:]
 LAG = 2
-GATE = 3
+GATE = 2
 FLOW = ("mid", "near", "far", "own")
 N_SEM = 208
 
@@ -65,7 +65,7 @@
 
 def kernel(
     acts, grads, routes_f, routes_b, gates_f, gates_b, w_gate, w_up, w_down, stash,
-    out_f, out_b,
+    out_f, ends,
     rows, part, back, slots, toks, named, scale, sums, gets, wgu, wd, st, acc,
     send_sem, recv_sem, local_sem, go,
 ):
@@ -455,7 +455,7 @@
 
             tiled(two)
             own[name] = local(part.at[8 * r + z], back.at[8 * r + z])
-            for d in ORDER[1:]:
+            for d in ORDER[:0:-1]:
                 send(("p", name, d), part.at[8 * r + at_z(-d)], back.at[8 * r + z], dev(-d, 0, 1))
 
         def combine(name):
@@ -466,27 +466,27 @@
             for c, table in enumerate(tables(r)):
                 table = plain(table)
                 if name == "near":
-                    arrive(("e1", c), gets.at[2 + c])
+                    arrive(("e1", c), gets.at[c])
                 if name == "own":
-                    arrive(("e2", c), gets.at[4 + c])
+                    arrive(("e2", c), gets.at[2 + c])
 
                 def step(cols):
                     total = lead(table, back[pl.ds(8 * r, NZ), :, cols].reshape(SLOTS, TILE))
                     if name == "near":
-                        total = total + gets[2 + c, :, cols].astype(F32)
+                        total = total + gets[c, :, cols].astype(F32)
                     if name == "own":
-                        total = total + gets[4 + c, :, cols].astype(F32) + toks[0, c, :, cols].astype(F32)
+                        total = total + gets[2 + c, :, cols].astype(F32) + toks[0, c, :, cols].astype(F32)
                     sums[r, c, :, cols] = total.astype(BF)
 
                 tiled(step)
                 if name == "far":
-                    send(("e1", c), sums.at[r, c], gets.at[2 + c], dev(0, side, 1))
+                    send(("e1", c), sums.at[r, c], gets.at[c], dev(0, side, 1))
                 if name == "mid":
-                    send(("e2", c), sums.at[r, c], gets.at[4 + c], dev(0, -side, 1))
+                    send(("e2", c), sums.at[r, c], gets.at[2 + c], dev(0, -side, 1))
                 if name == "near":
-                    send("end1", sums.at[r, c], gets.at[1], dev(0, side, c, pp_next), c)
+                    send("end1", sums.at[r, c], ends.at[1], dev(0, side, c, pp_next), c)
                 if name == "own":
-                    send("end0", sums.at[r, c], gets.at[0], dev(0, 0, c, pp_next), c)
+                    send("end0", sums.at[r, c], ends.at[0], dev(0, 0, c, pp_next), c)
 
         order = ("far", "mid", "near", "own")
         for name in FLOW:
@@ -496,28 +496,22 @@
         arrive("out", out_f.at[0])
         sent()
 
-    arrive("end1", gets.at[1])
-    arrive("end0", gets.at[0])
-
-    def total(cols):
-        out_b[0, :, cols] = (gets[0, :, cols].astype(F32) + gets[1, :, cols].astype(F32)).astype(BF)
-
-    tiled(total)
+    arrive("end1", ends.at[1])
+    arrive("end0", ends.at[0])
     assert len(ids) <= N_SEM
 
 
 def on_device(acts, grads, routes_f, routes_b, gates_f, gates_b, w_gate, w_up, w_down, stash):
     width = acts.shape[2]
     anywhere = pl.BlockSpec(memory_space=pl.ANY)
-    inside = pl.BlockSpec(memory_space=pltpu.VMEM)
     out = jax.ShapeDtypeStruct((1, TOK, width), BF)
     chunks = pltpu.VMEM((NZ * NY, PAIR, width), BF)
-    return pl.pallas_call(
+    out, ends = pl.pallas_call(
         kernel,
         name="relay",
-        out_shape=(out, out),
+        out_shape=(out, jax.ShapeDtypeStruct((2, TOK, width), BF)),
         in_specs=[anywhere] * 10,
-        out_specs=(anywhere, inside),
+        out_specs=(anywhere, anywhere),
         scratch_shapes=[
             chunks,
             chunks,
@@ -527,7 +521,7 @@
             pltpu.VMEM((NY, 2, 2, TOK), jnp.int32),
             pltpu.VMEM((NY, 2, 2, TOK), F32),
             pltpu.VMEM((NY, 2, TOK, width), BF),
-            pltpu.VMEM((6, TOK, width), BF),
+            pltpu.VMEM((4, TOK, width), BF),
             pltpu.VMEM((width, 512), BF),
             pltpu.VMEM((256, width), BF),
             pltpu.VMEM((2, NZ, NY, 32, 128), BF),
@@ -544,6 +538,7 @@
         acts, grads, routes_f[0].T, routes_b[0].T, gates_f[0].T, gates_b[0].T,
         w_gate, w_up, w_down, stash.reshape(NZ, NY, 32, 128),
     )
+    return out, (ends[0:1].astype(F32) + ends[1:2].astype(F32)).astype(BF)
 
 
 def solution(mesh):

time: 128 us -> 125 us (0.977)
  the two profiles are of different devices: /device:TPU:12 before, /device:TPU:29 now
where the time goes in v3:
time: 125 us
  Pallas kernels  122 us (98%)
  other arithmetic  1.75 us (1%)
    pallas_call x1, Pallas kernels, on_device(): pl.pallas_call(kernel, name='relay', out_shape=(out, jax.ShapeDtypeStruct...  122 us

profile of v3, /device:TPU:29, one launch (start us, length us, event | category | flops | bytes accessed | tf_op | source)
XLA Modules:
  0.0 125.3 jit_solution(1303167398609351012)
XLA Ops:
  0.6 122.3 %relay.1 = (bf16[1,24,3584]{2,1,0:T(8,128)(2,1)}, bf16[2,24,3584]{2,1,0:T(8,128)(2,1)}) custom-call(bf16[1,24,3584]{2,1,0:T(8,128)(2,1)} %acts.1, bf16[1,24,3584]{2,1,0:T(8,128)(2,1)} %grads.1, s32[2,24]{1,0:T(2,128)} %bitcast.14, s32[2,24]{1,0:T(2,128)} %bitcast.15, f32[2,24]{1,0:T(2,128)} %bitcast.16, f32[2,24]{1,0:T(2,128)} %bitcast.17, ...), custom_call_target="tpu_custom_call" | custom-call | tf_op jit(solution)/shard_map/relay/pallas_call | solution.py:509
  122.9 0.0 copy-start
  122.9 1.7 %add_convert_fusion = bf16[1,24,3584]{2,1,0:T(8,128)(2,1)} fusion(bf16[2,24,3584]{2,1,0:T(8,128)(2,1)} %get-tuple-element.5), kind=kLoop, calls=%fused_computation | loop fusion | flops 344064 | bytes 516096 | tf_op jit(solution)/shard_map/convert_element_type | solution.py:541
  124.7 0.0 copy-done
  124.7 0.7 copy.13
Async XLA Ops:
  122.9 1.8 %copy-start = (bf16[1,24,3584]{2,1,0:T(8,128)(2,1)S(1)}, bf16[1,24,3584]{2,1,0:T(8,128)(2,1)}, u32[]{:S(2)}) copy-start(bf16[1,24,3584]{2,1,0:T(8,128)(2,1)} %get-tuple-element.8) | copy-start | bytes 516100

commit v4 on v3

--- a/solution.py
+++ b/solution.py
@@ -71,6 +71,7 @@
 ):
     width = rows.shape[2]
     tiles = width // TILE
+    cuts = ((0, tiles // 2), (tiles // 2, tiles))
     pp, ep = lax.axis_index("pp"), lax.axis_index("ep")
     n_pp = lax.axis_size("pp")
     z, y, core = ep // 8, lax.rem(ep, 8) // 2, lax.rem(ep, 2)
@@ -120,8 +121,8 @@
         copy.start()
         return copy
 
-    def tiled(step):
-        lax.fori_loop(0, tiles, lambda i, _: (step(pl.ds(pl.multiple_of(i * TILE, TILE), TILE)), 0)[1], 0)
+    def tiled(step, first=0, last=tiles):
+        lax.fori_loop(first, last, lambda i, _: (step(pl.ds(pl.multiple_of(i * TILE, TILE), TILE)), 0)[1], 0)
 
     barrier = pltpu.get_barrier_semaphore()
 
@@ -478,6 +479,15 @@
                         total = total + gets[2 + c, :, cols].astype(F32) + toks[0, c, :, cols].astype(F32)
                     sums[r, c, :, cols] = total.astype(BF)
 
+                if name == "own":
+                    for n, (first, last) in enumerate(cuts):
+                        tiled(step, first, last)
+                        cols = pl.ds(first * TILE, (last - first) * TILE)
+                        send(
+                            ("end0", n), sums.at[r, c, :, cols], ends.at[0, :, cols],
+                            dev(0, 0, c, pp_next), c,
+                        )
+                    continue
                 tiled(step)
                 if name == "far":
                     send(("e1", c), sums.at[r, c], gets.at[c], dev(0, side, 1))
@@ -485,8 +495,6 @@
                     send(("e2", c), sums.at[r, c], gets.at[2 + c], dev(0, -side, 1))
                 if name == "near":
                     send("end1", sums.at[r, c], ends.at[1], dev(0, side, c, pp_next), c)
-                if name == "own":
-                    send("end0", sums.at[r, c], ends.at[0], dev(0, 0, c, pp_next), c)
 
         order = ("far", "mid", "near", "own")
         for name in FLOW:
@@ -497,7 +505,8 @@
         sent()
 
     arrive("end1", ends.at[1])
-    arrive("end0", ends.at[0])
+    for n, (first, last) in enumerate(cuts):
+        arrive(("end0", n), ends.at[0, :, pl.ds(first * TILE, (last - first) * TILE)])
     assert len(ids) <= N_SEM
 
 

time: 125 us -> 125 us (level)
  no operation moved by 1% of the time
where the time goes in v4:
time: 125 us
  Pallas kernels  122 us (98%)
  other arithmetic  1.75 us (1%)
    pallas_call x1, Pallas kernels, on_device(): pl.pallas_call(kernel, name='relay', out_shape=(out, jax.ShapeDtypeStruct...  122 us

profile of v4, /device:TPU:29, one launch (start us, length us, event | category | flops | bytes accessed | tf_op | source)
XLA Modules:
  0.0 124.6 jit_solution(14343081419832870076)
XLA Ops:
  0.6 121.5 %relay.1 = (bf16[1,24,3584]{2,1,0:T(8,128)(2,1)}, bf16[2,24,3584]{2,1,0:T(8,128)(2,1)}) custom-call(bf16[1,24,3584]{2,1,0:T(8,128)(2,1)} %acts.1, bf16[1,24,3584]{2,1,0:T(8,128)(2,1)} %grads.1, s32[2,24]{1,0:T(2,128)} %bitcast.14, s32[2,24]{1,0:T(2,128)} %bitcast.15, f32[2,24]{1,0:T(2,128)} %bitcast.16, f32[2,24]{1,0:T(2,128)} %bitcast.17, ...), custom_call_target="tpu_custom_call" | custom-call | tf_op jit(solution)/shard_map/relay/pallas_call | solution.py:518
  122.2 0.0 copy-start
  122.2 1.7 %add_convert_fusion = bf16[1,24,3584]{2,1,0:T(8,128)(2,1)} fusion(bf16[2,24,3584]{2,1,0:T(8,128)(2,1)} %get-tuple-element.5), kind=kLoop, calls=%fused_computation | loop fusion | flops 344064 | bytes 516096 | tf_op jit(solution)/shard_map/convert_element_type | solution.py:550
  123.9 0.0 copy-done
  123.9 0.7 copy.13
Async XLA Ops:
  122.2 1.8 %copy-start = (bf16[1,24,3584]{2,1,0:T(8,128)(2,1)S(1)}, bf16[1,24,3584]{2,1,0:T(8,128)(2,1)}, u32[]{:S(2)}) copy-start(bf16[1,24,3584]{2,1,0:T(8,128)(2,1)} %get-tuple-element.8) | copy-start | bytes 516100
